TPU v7x, 256 devices: a whole 4x4x8 slice. The times are simulated.
256 devices in a mesh: seq: 32 (over x_lo, z, core), resp: 8 (over y, x_hi).
Axes of the slice: x: 4 (x_hi: 2, x_lo: 2; x = x_hi * 2 + x_lo), y: 4, z: 8, core: 2. Of those that a mesh axis runs over, the one named last changes fastest.
Arguments:
- queries: bfloat16 [8, 4096, 4096], P('resp', 'seq'), may hold values from -7 to 7
- resp_keys: bfloat16 [8, 4096, 1024], P('resp', 'seq'), may hold values from -6 to 6
- resp_values: bfloat16 [8, 4096, 1024], P('resp', 'seq'), may hold values from -6 to 6
- prompt_keys: bfloat16 [2, 1024, 1024], P(None, 'seq'), may hold values from -4 to 4
- prompt_values: bfloat16 [2, 1024, 1024], P(None, 'seq'), may hold values from -6 to 6
- response_prompt: int32 [32], replicated, may hold values from 0 to 1, as said below
- out_grad: bfloat16 [8, 4096, 4096], P('resp', 'seq'), may hold values from -6 to 6
Outputs:
- attended: bfloat16 [8, 4096, 4096], P('resp', 'seq')
- query_grad: bfloat16 [8, 4096, 4096], P('resp', 'seq')
- resp_key_grad: bfloat16 [8, 4096, 1024], P('resp', 'seq')
- resp_value_grad: bfloat16 [8, 4096, 1024], P('resp', 'seq')
- prompt_key_grad: bfloat16 [2, 1024, 1024], P(None, 'seq')
- prompt_value_grad: bfloat16 [2, 1024, 1024], P(None, 'seq')
Inputs may be any that keep to these rules, and one draw needn't show every extreme that they name: `response_prompt`: each of the 2 prompts has at least one response.
All inputs are finite; a program needn't handle non-finite values.
Results may differ from a plain program's by a relative error of at most 0.0051.
Values may be sent and summed in bfloat16 or wider, within the bound.
A program may use at most 128 MiB of HBM per device.

v0:
```python
import math

import jax
import jax.numpy as jnp
from jax import lax
from jax.sharding import PartitionSpec as P

H = 32
KVH = 8
HD = 128
SPAN = 128
RLEN = 1024
PROMPTS = 2
PDEV = 32


def from_behind(x, axis, by):
    devices = lax.axis_size(axis)
    pairs = [(i, i + by) for i in range(devices) if 0 <= i + by < devices]
    return lax.ppermute(x, axis, pairs)


def head_pass(query_head, key_head, value_head, grad_head, allowed, scaling):
    scores = (
        jnp.einsum("qgd,kd->gqk", query_head, key_head, preferred_element_type=jnp.float32)
        * scaling
    )
    scores = jnp.where(allowed[None], scores, -jnp.inf)
    top_score = jnp.max(scores, axis=2, keepdims=True)
    weights = jnp.exp(scores - top_score)
    probs = weights / jnp.sum(weights, axis=2, keepdims=True)
    probs_low = probs.astype(jnp.bfloat16)
    attended = jnp.einsum(
        "gqk,kd->qgd", probs_low, value_head, preferred_element_type=jnp.float32
    ).astype(jnp.bfloat16)
    prob_grad = jnp.einsum("qgd,kd->gqk", grad_head, value_head, preferred_element_type=jnp.float32)
    centre = jnp.sum(probs * prob_grad, axis=2, keepdims=True)
    score_grad = (probs * (prob_grad - centre)).astype(jnp.bfloat16)
    query_grad = (
        jnp.einsum("gqk,kd->qgd", score_grad, key_head, preferred_element_type=jnp.float32)
        * scaling
    ).astype(jnp.bfloat16)
    key_grad = (
        jnp.einsum("gqk,qgd->kd", score_grad, query_head, preferred_element_type=jnp.float32)
        * scaling
    )
    value_grad = jnp.einsum("gqk,qgd->kd", probs_low, grad_head, preferred_element_type=jnp.float32)
    return (attended, query_grad, key_grad, value_grad)


def body(queries, resp_keys, resp_values, prompt_keys, prompt_values, response_prompt, out_grad):
    scaling = 1.0 / math.sqrt(HD)
    group_size = H // KVH
    kv_width = KVH * HD
    span_count = RLEN // SPAN
    seq_count = lax.axis_size("seq")
    seq_pos = lax.axis_index("seq")
    span_here = seq_pos % span_count
    resp_here = lax.axis_index("resp") * (seq_count // span_count) + seq_pos // span_count
    prompt_here = response_prompt[resp_here]
    both_prompt = (
        lax.all_gather(prompt_keys, "seq", axis=1, tiled=True),
        lax.all_gather(prompt_values, "seq", axis=1, tiled=True),
    )
    prompt_len = both_prompt[0].shape[1]
    prompt_key = lax.dynamic_index_in_dim(both_prompt[0], prompt_here, 0, False)
    prompt_value = lax.dynamic_index_in_dim(both_prompt[1], prompt_here, 0, False)
    own_pair = jnp.concatenate([resp_keys[0], resp_values[0]], axis=1)
    slot_list = [own_pair for slot_index in range(span_count)]
    for distance in range(1, span_count):
        slot_list[span_count - 1 - distance] = from_behind(own_pair, "seq", distance)
    window = jnp.stack(slot_list, axis=0)
    window = window.reshape(RLEN, 2 * kv_width)
    key_full = jnp.concatenate([prompt_key, window[:, :kv_width]], axis=0).reshape(
        prompt_len + RLEN, KVH, HD
    )
    value_full = jnp.concatenate([prompt_value, window[:, kv_width:]], axis=0).reshape(
        prompt_len + RLEN, KVH, HD
    )
    query_pos = span_here * SPAN + jnp.arange(SPAN)
    key_pos = (span_here - span_count + 1) * SPAN + jnp.arange(RLEN)
    resp_allowed = (key_pos[None, :] >= 0) & (key_pos[None, :] <= query_pos[:, None])
    allowed = jnp.concatenate([jnp.ones((SPAN, prompt_len), bool), resp_allowed], axis=1)
    query_heads = queries[0].reshape(SPAN, KVH, group_size, HD).transpose(1, 0, 2, 3)
    grad_heads = out_grad[0].reshape(SPAN, KVH, group_size, HD).transpose(1, 0, 2, 3)

    def per_head(head_inputs):
        return head_pass(
            head_inputs[0], head_inputs[1], head_inputs[2], head_inputs[3], allowed, scaling
        )

    attended, query_grad, key_grad, value_grad = lax.map(
        per_head,
        (query_heads, key_full.transpose(1, 0, 2), value_full.transpose(1, 0, 2), grad_heads),
    )
    attended = attended.transpose(1, 0, 2, 3).reshape(1, SPAN, H * HD)
    query_grad = query_grad.transpose(1, 0, 2, 3).reshape(1, SPAN, H * HD)
    key_grad = key_grad.transpose(1, 0, 2).reshape(prompt_len + RLEN, kv_width)
    value_grad = value_grad.transpose(1, 0, 2).reshape(prompt_len + RLEN, kv_width)
    onehot = (jnp.arange(PROMPTS) == prompt_here).astype(jnp.float32)
    pair_rows = jnp.concatenate([key_grad[:prompt_len], value_grad[:prompt_len]], axis=1)
    grad_term = (onehot[None, :, None] * pair_rows[:, None, :]).reshape(
        prompt_len, PROMPTS * 2 * kv_width
    )
    prompt_share = lax.psum_scatter(grad_term, "seq", scatter_dimension=0, tiled=True)
    prompt_share = lax.psum(prompt_share, "resp")
    prompt_share = prompt_share.reshape(PDEV, PROMPTS, 2, kv_width).transpose(1, 2, 0, 3)
    prompt_key_grad = prompt_share[:, 0].astype(jnp.bfloat16)
    prompt_value_grad = prompt_share[:, 1].astype(jnp.bfloat16)
    grad_parts = jnp.concatenate([key_grad[prompt_len:], value_grad[prompt_len:]], axis=1).reshape(
        span_count, SPAN, 2 * kv_width
    )
    summed = grad_parts[span_count - 1]
    for distance in range(1, span_count):
        summed = summed + from_behind(grad_parts[span_count - 1 - distance], "seq", -distance)
    resp_key_grad = summed[:, :kv_width].astype(jnp.bfloat16)[None]
    resp_value_grad = summed[:, kv_width:].astype(jnp.bfloat16)[None]
    return (
        attended,
        query_grad,
        resp_key_grad,
        resp_value_grad,
        prompt_key_grad,
        prompt_value_grad,
    )


def solution(mesh):
    return jax.shard_map(
        body,
        mesh=mesh,
        in_specs=(
            P("resp", "seq", None),
            P("resp", "seq", None),
            P("resp", "seq", None),
            P(None, "seq", None),
            P(None, "seq", None),
            P(),
            P("resp", "seq", None),
        ),
        out_specs=(
            P("resp", "seq", None),
            P("resp", "seq", None),
            P("resp", "seq", None),
            P("resp", "seq", None),
            P(None, "seq", None),
            P(None, "seq", None),
        ),
        check_vma=False,
    )
```

profile of v0, /device:TPU:6, one launch (start us, length us, event | category | flops | bytes accessed | tf_op | source)
XLA Modules:
  0.0 957.6 jit_solution(3366102891497787584)
XLA Ops:
  10.9 6.0 collective-permute-start
  16.9 5.9 collective-permute-start.1
  37.6 9.5 collective-permute-done
  47.1 46.9 %collective-permute-start.5 = (bf16[128,2048]{1,0:T(8,128)(2,1)S(1)}, bf16[128,2048]{1,0:T(8,128)(2,1)S(1)}, u32[]{:S(2)}, u32[]{:S(2)}) collective-permute-start(bf16[128,2048]{1,0:T(8,128)(2,1)S(1)} %pad_maximum_fusion.2), channel_id=1, source_target_pairs={{0,16},{8,24},{16,32},{24,40},{32,48},{40,56},{48,64},{56,72},{64,... | collective-permute-start | bytes 1572872 | tf_op jit(solution)/shard_map/ppermute | solution.py:20
  95.1 26.2 %collective-permute-done.1 = bf16[128,2048]{1,0:T(8,128)(2,1)} collective-permute-done((bf16[128,2048]{1,0:T(8,128)(2,1)S(1)}, bf16[128,2048]{1,0:T(8,128)(2,1)}, u32[]{:S(2)}, u32[]{:S(2)}) %collective-permute-start.1) | collective-permute-done | bytes 524320 | tf_op jit(solution)/shard_map/ppermute | solution.py:20
  125.4 33.4 %collective-permute-done.3 = bf16[128,2048]{1,0:T(8,128)(2,1)} collective-permute-done((bf16[128,2048]{1,0:T(8,128)(2,1)S(1)}, bf16[128,2048]{1,0:T(8,128)(2,1)}, u32[]{:S(2)}, u32[]{:S(2)}) %collective-permute-start.3) | collective-permute-done | bytes 524320 | tf_op jit(solution)/shard_map/ppermute | solution.py:20
  159.9 11.5 %collective-permute-done.4 = bf16[128,2048]{1,0:T(8,128)(2,1)S(1)} collective-permute-done((bf16[128,2048]{1,0:T(8,128)(2,1)S(1)}, bf16[128,2048]{1,0:T(8,128)(2,1)S(1)}, u32[]{:S(2)}, u32[]{:S(2)}) %collective-permute-start.4) | collective-permute-done | bytes 524320 | tf_op jit(solution)/shard_map/ppermute | solution.py:20
  179.9 8.5 constant_dynamic-slice_fusion
  188.4 10.6 %copy.104 = bf16[1,1024,1024]{1,2,0:T(8,128)(2,1)} copy(bf16[1,1024,1024]{2,0,1:T(2,128)(2,1)} %constant_dynamic-slice_fusion) | data formatting | bytes 4194304
  199.0 42.0 %all-gather.3.cloned.1.call-done = bf16[2,1024,1024]{2,1,0:T(8,128)(2,1)} async-done(((bf16[2,32,1024]{2,1,0:T(8,128)(2,1)}), bf16[2,1024,1024]{2,1,0:T(8,128)(2,1)}) %all-gather.3.cloned.1.call-update) | async-done | bytes 4194320 | tf_op jit(solution)/shard_map/all_gather | solution.py:63
  245.4 5.9 maximum_bitcast_fusion
  251.3 187.4 %while.16 = (s32[]{:T(128)}, bf16[8,128,4,128]{1,3,2,0:T(8,128)(2,1)}, bf16[8,128,4,128]{1,3,2,0:T(8,128)(2,1)}, f32[8,2048,128]{1,2,0:T(8,128)}, f32[8,2048,128...) while((s32[]{:T(128)}, ...), condition=%wide.region_4.5_spmd, body=%wide.region_0.4_spmd.sunk | while | flops 2169969152 | bytes 63723204 | solution.py:92
  438.7 6.7 fusion.94
  445.4 6.7 fusion.95
  456.2 9.2 copy.84
  465.4 11.8 %mul.54 = f32[1024,2,2048]{2,1,0:T(2,128)} broadcast(f32[1024,2048]{1,0:T(8,128)} %copy.84), dimensions={0,2} | broadcast | bytes 25165824 | tf_op jit(solution)/shard_map/mul | solution.py:102
  477.2 19.3 %copy.107 = f32[128,8,2,2048]{3,1,2,0:T(8,128)S(1)} copy(f32[128,8,2,2048]{3,2,1,0:T(2,128)} %bitcast.226) | data formatting | bytes 33554432
  496.5 6.2 broadcast_multiply_fusion
  502.7 5.4 copy.82
  508.1 5.4 copy.83
  513.5 5.6 fusion.83
  519.1 5.3 collective-permute-start.10
  535.4 47.0 %collective-permute-done.10 = f32[128,2048]{1,0:T(8,128)S(1)} collective-permute-done((f32[128,2048]{1,0:T(8,128)S(1)}, f32[128,2048]{1,0:T(8,128)S(1)}, u32[]{:S(2)}, u32[]{:S(2)}) %collective-permute-start.10) | collective-permute-done | bytes 1048608 | tf_op jit(solution)/shard_map/ppermute | solution.py:20
  582.4 7.1 collective-permute-start.8
  589.5 57.4 %collective-permute-done.11 = f32[128,2048]{1,0:T(8,128)S(1)} collective-permute-done((f32[128,2048]{1,0:T(8,128)S(1)}, f32[128,2048]{1,0:T(8,128)S(1)}, u32[]{:S(2)}, u32[]{:S(2)}) %collective-permute-start.11) | collective-permute-done | bytes 1048608 | tf_op jit(solution)/shard_map/ppermute | solution.py:20
  646.9 39.0 %collective-permute-start.9 = (f32[128,2048]{1,0:T(8,128)}, f32[128,2048]{1,0:T(8,128)}, u32[]{:S(2)}, u32[]{:S(2)}) collective-permute-start(f32[128,2048]{1,0:T(8,128)} %get-tuple-element.131), channel_id=1, source_target_pairs={{24,0},{32,8},{40,16},{48,24},{56,32},{64,40},{72,48},{80,56},{88,... | collective-permute-start | bytes 3145736 | tf_op jit(solution)/shard_map/ppermute | solution.py:20
  690.5 37.9 %collective-permute-done.12 = f32[128,2048]{1,0:T(8,128)S(1)} collective-permute-done((f32[128,2048]{1,0:T(8,128)}, f32[128,2048]{1,0:T(8,128)S(1)}, u32[]{:S(2)}, u32[]{:S(2)}) %collective-permute-start.12) | collective-permute-done | bytes 1048608 | tf_op jit(solution)/shard_map/ppermute | solution.py:20
  728.3 59.9 %collective-permute-done.13 = f32[128,2048]{1,0:T(8,128)} collective-permute-done((f32[128,2048]{1,0:T(8,128)}, f32[128,2048]{1,0:T(8,128)}, u32[]{:S(2)}, u32[]{:S(2)}) %collective-permute-start.13) | collective-permute-done | bytes 1048608 | tf_op jit(solution)/shard_map/ppermute | solution.py:20
  788.2 12.1 %collective-permute-done.7 = f32[128,2048]{1,0:T(8,128)} collective-permute-done((f32[128,2048]{1,0:T(8,128)}, f32[128,2048]{1,0:T(8,128)}, u32[]{:S(2)}, u32[]{:S(2)}) %collective-permute-start.7) | collective-permute-done | bytes 1048608 | tf_op jit(solution)/shard_map/ppermute | solution.py:20
  800.3 69.2 %collective-permute-done.8 = f32[128,2048]{1,0:T(8,128)} collective-permute-done((f32[128,2048]{1,0:T(8,128)}, f32[128,2048]{1,0:T(8,128)}, u32[]{:S(2)}, u32[]{:S(2)}) %collective-permute-start.8) | collective-permute-done | bytes 1048608 | tf_op jit(solution)/shard_map/ppermute | solution.py:20
  873.6 27.6 %reduce-scatter.2.cloned.1.call-done = f32[32,4096]{1,0:T(8,128)} async-done(((f32[1024,4096]{1,0:T(8,128)}), f32[32,4096]{1,0:T(8,128)}) %reduce-scatter.2.cloned.1.call-update) | async-done | bytes 524304 | tf_op jit(solution)/shard_map/reduce_scatter | solution.py:105
  902.6 46.6 %all-reduce.2 = bf16[2,2,32,1024]{3,1,0,2:T(2,128)(2,1)S(1)} all-reduce(f32[2,2,32,1024]{3,1,0,2:T(2,128)S(1)} %bitcast.240), channel_id=1, replica_groups=mesh['seq'=32,'resp'=8] {'resp'}, use_global_device_ids=true, to_apply=%region_6.7 | all-reduce | flops 131072 | bytes 786432 | tf_op jit(solution)/shard_map/psum | solution.py:106
  (186 shorter events, 249.7 us)
Async XLA Ops:
  7.2 27.8 %copy-start.3 = (bf16[1,128,4096]{2,1,0:T(8,128)(2,1)S(1)}, bf16[1,128,4096]{2,1,0:T(8,128)(2,1)}, u32[]{:S(2)}) copy-start(bf16[1,128,4096]{2,1,0:T(8,128)(2,1)} %param.15) | copy-start | bytes 3145732
  7.2 172.8 %all-gather.5.cloned.1.call-start = ((), (), s32[]{:S(2)}) async-start(), calls=%async_computation.2 | async-start | bytes 4325376 | tf_op jit(solution)/shard_map/all_gather | solution.py:62
  9.0 231.9 %all-gather.3.cloned.1.call-start = ((), (), s32[]{:S(2)}) async-start(), calls=%async_computation.1 | async-start | bytes 4325376 | tf_op jit(solution)/shard_map/all_gather | solution.py:63
  9.8 891.4 %reduce-scatter.2.cloned.1.call-start = ((), (), s32[]{:S(2)}) async-start(), calls=%async_computation.3 | async-start | bytes 17301504 | tf_op jit(solution)/shard_map/reduce_scatter | solution.py:105
  10.9 36.2 %collective-permute-start = (bf16[128,2048]{1,0:T(8,128)(2,1)S(1)}, bf16[128,2048]{1,0:T(8,128)(2,1)}, u32[]{:S(2)}, u32[]{:S(2)}) collective-permute-start(bf16[128,2048]{1,0:T(8,128)(2,1)S(1)} %pad_maximum_fusion.2), channel_id=1, source_target_pairs={{0,56},{8,64},{16,72},{24,80},{32,88},{40,96},{48,104},{56,112},{6... | collective-permute-start | bytes 1572872 | tf_op jit(solution)/shard_map/ppermute | solution.py:20
  16.9 104.4 %collective-permute-start.1 = (bf16[128,2048]{1,0:T(8,128)(2,1)S(1)}, bf16[128,2048]{1,0:T(8,128)(2,1)}, u32[]{:S(2)}, u32[]{:S(2)}) collective-permute-start(bf16[128,2048]{1,0:T(8,128)(2,1)S(1)} %pad_maximum_fusion.2), channel_id=1, source_target_pairs={{0,48},{8,56},{16,64},{24,72},{32,80},{40,88},{48,96},{56,104},{64... | collective-permute-start | bytes 1572872 | tf_op jit(solution)/shard_map/ppermute | solution.py:20
  22.8 101.4 %collective-permute-start.2 = (bf16[128,2048]{1,0:T(8,128)(2,1)S(1)}, bf16[128,2048]{1,0:T(8,128)(2,1)}, u32[]{:S(2)}, u32[]{:S(2)}) collective-permute-start(bf16[128,2048]{1,0:T(8,128)(2,1)S(1)} %pad_maximum_fusion.2), channel_id=1, source_target_pairs={{0,40},{8,48},{16,56},{24,64},{32,72},{40,80},{48,88},{56,96},{64,... | collective-permute-start | bytes 1572872 | tf_op jit(solution)/shard_map/ppermute | solution.py:20
  25.0 133.8 %collective-permute-start.3 = (bf16[128,2048]{1,0:T(8,128)(2,1)S(1)}, bf16[128,2048]{1,0:T(8,128)(2,1)}, u32[]{:S(2)}, u32[]{:S(2)}) collective-permute-start(bf16[128,2048]{1,0:T(8,128)(2,1)S(1)} %pad_maximum_fusion.2), channel_id=1, source_target_pairs={{0,32},{8,40},{16,48},{24,56},{32,64},{40,72},{48,80},{56,88},{64,... | collective-permute-start | bytes 1572872 | tf_op jit(solution)/shard_map/ppermute | solution.py:20
  27.0 144.4 %collective-permute-start.4 = (bf16[128,2048]{1,0:T(8,128)(2,1)S(1)}, bf16[128,2048]{1,0:T(8,128)(2,1)S(1)}, u32[]{:S(2)}, u32[]{:S(2)}) collective-permute-start(bf16[128,2048]{1,0:T(8,128)(2,1)S(1)} %pad_maximum_fusion.2), channel_id=1, source_target_pairs={{0,24},{8,32},{16,40},{24,48},{32,56},{40,64},{48,72},{56,80},{64,... | collective-permute-start | bytes 1572872 | tf_op jit(solution)/shard_map/ppermute | solution.py:20
  36.3 135.2 %copy-start.4 = (bf16[1,128,1024]{2,1,0:T(8,128)(2,1)S(1)}, bf16[1,128,1024]{2,1,0:T(8,128)(2,1)}, u32[]{:S(2)}) copy-start(bf16[1,128,1024]{2,1,0:T(8,128)(2,1)} %param.11) | copy-start | bytes 786436
  36.3 135.2 %copy-start.5 = (bf16[1,128,1024]{2,1,0:T(8,128)(2,1)S(1)}, bf16[1,128,1024]{2,1,0:T(8,128)(2,1)}, u32[]{:S(2)}) copy-start(bf16[1,128,1024]{2,1,0:T(8,128)(2,1)} %param.10) | copy-start | bytes 786436
  47.1 124.3 %collective-permute-start.5 = (bf16[128,2048]{1,0:T(8,128)(2,1)S(1)}, bf16[128,2048]{1,0:T(8,128)(2,1)S(1)}, u32[]{:S(2)}, u32[]{:S(2)}) collective-permute-start(bf16[128,2048]{1,0:T(8,128)(2,1)S(1)} %pad_maximum_fusion.2), channel_id=1, source_target_pairs={{0,16},{8,24},{16,32},{24,40},{32,48},{40,56},{48,64},{56,72},{64,... | collective-permute-start | bytes 1572872 | tf_op jit(solution)/shard_map/ppermute | solution.py:20
  121.3 50.2 %collective-permute-start.6 = (bf16[128,2048]{1,0:T(8,128)(2,1)S(1)}, bf16[128,2048]{1,0:T(8,128)(2,1)S(1)}, u32[]{:S(2)}, u32[]{:S(2)}) collective-permute-start(bf16[128,2048]{1,0:T(8,128)(2,1)S(1)} %pad_maximum_fusion.2), channel_id=1, source_target_pairs={{0,8},{8,16},{16,24},{24,32},{32,40},{40,48},{48,56},{56,64},{64,7... | collective-permute-start | bytes 1572872 | tf_op jit(solution)/shard_map/ppermute | solution.py:20
  251.3 8.9 copy-start.1
  266.8 4.2 copy-start.2
  274.8 8.9 copy-start.1
  298.2 8.9 copy-start.1
  321.6 8.9 copy-start.1
  337.1 4.2 copy-start.2
  345.0 8.9 copy-start.1
  360.5 4.2 copy-start.2
  368.4 8.9 copy-start.1
  391.9 8.9 copy-start.1
  415.3 8.9 copy-start.1
  477.2 19.4 %copy-start.6 = (f32[1,16,2,128]{3,1,2,0:T(8,128)S(1)}, f32[1,16,2,128]{3,1,2,0:T(8,128)}, u32[]{:S(2)}) copy-start(f32[1,16,2,128]{3,1,2,0:T(8,128)} %copy.106) | copy-start | bytes 49156
  519.1 63.4 %collective-permute-start.10 = (f32[128,2048]{1,0:T(8,128)S(1)}, f32[128,2048]{1,0:T(8,128)S(1)}, u32[]{:S(2)}, u32[]{:S(2)}) collective-permute-start(f32[128,2048]{1,0:T(8,128)S(1)} %get-tuple-element.132), channel_id=1, source_target_pairs={{32,0},{40,8},{48,16},{56,24},{64,32},{72,40},{80,48},{88,56},{96,... | collective-permute-start | bytes 3145736 | tf_op jit(solution)/shard_map/ppermute | solution.py:20
  524.4 122.6 %collective-permute-start.11 = (f32[128,2048]{1,0:T(8,128)S(1)}, f32[128,2048]{1,0:T(8,128)S(1)}, u32[]{:S(2)}, u32[]{:S(2)}) collective-permute-start(f32[128,2048]{1,0:T(8,128)S(1)} %get-tuple-element.133), channel_id=1, source_target_pairs={{40,0},{48,8},{56,16},{64,24},{72,32},{80,40},{88,48},{96,56},{104... | collective-permute-start | bytes 3145736 | tf_op jit(solution)/shard_map/ppermute | solution.py:20
  528.5 199.8 %collective-permute-start.12 = (f32[128,2048]{1,0:T(8,128)}, f32[128,2048]{1,0:T(8,128)S(1)}, u32[]{:S(2)}, u32[]{:S(2)}) collective-permute-start(f32[128,2048]{1,0:T(8,128)} %get-tuple-element.135), channel_id=1, source_target_pairs={{48,0},{56,8},{64,16},{72,24},{80,32},{88,40},{96,48},{104,56},{11... | collective-permute-start | bytes 3145736 | tf_op jit(solution)/shard_map/ppermute | solution.py:20
  531.1 257.1 %collective-permute-start.13 = (f32[128,2048]{1,0:T(8,128)}, f32[128,2048]{1,0:T(8,128)}, u32[]{:S(2)}, u32[]{:S(2)}) collective-permute-start(f32[128,2048]{1,0:T(8,128)} %get-tuple-element.134), channel_id=1, source_target_pairs={{56,0},{64,8},{72,16},{80,24},{88,32},{96,40},{104,48},{112,56},{1... | collective-permute-start | bytes 3145736 | tf_op jit(solution)/shard_map/ppermute | solution.py:20
  533.2 267.1 %collective-permute-start.7 = (f32[128,2048]{1,0:T(8,128)}, f32[128,2048]{1,0:T(8,128)}, u32[]{:S(2)}, u32[]{:S(2)}) collective-permute-start(f32[128,2048]{1,0:T(8,128)} %get-tuple-element.129), channel_id=1, source_target_pairs={{8,0},{16,8},{24,16},{32,24},{40,32},{48,40},{56,48},{64,56},{72,6... | collective-permute-start | bytes 3145736 | tf_op jit(solution)/shard_map/ppermute | solution.py:20
  582.4 287.1 %collective-permute-start.8 = (f32[128,2048]{1,0:T(8,128)}, f32[128,2048]{1,0:T(8,128)}, u32[]{:S(2)}, u32[]{:S(2)}) collective-permute-start(f32[128,2048]{1,0:T(8,128)} %get-tuple-element.130), channel_id=1, source_target_pairs={{16,0},{24,8},{32,16},{40,24},{48,32},{56,40},{64,48},{72,56},{80,... | collective-permute-start | bytes 3145736 | tf_op jit(solution)/shard_map/ppermute | solution.py:20
  646.9 222.6 %collective-permute-start.9 = (f32[128,2048]{1,0:T(8,128)}, f32[128,2048]{1,0:T(8,128)}, u32[]{:S(2)}, u32[]{:S(2)}) collective-permute-start(f32[128,2048]{1,0:T(8,128)} %get-tuple-element.131), channel_id=1, source_target_pairs={{24,0},{32,8},{40,16},{48,24},{56,32},{64,40},{72,48},{80,56},{88,... | collective-permute-start | bytes 3145736 | tf_op jit(solution)/shard_map/ppermute | solution.py:20
  (13 other events, 50.1 us)
Sparse Core Ops, SparseCore 0:
  10.4 156.3 all-gather.4
  168.7 72.2 all-gather.2
  502.8 398.2 reduce-scatter.1
where the time goes:
time: 966 us; the launch traced here: 958 us
  waiting for transfers between devices  434 us (45%)
  matrix products  159 us (16%)
  local copies, waits for them, and re-layouts  140 us (14%)
  starting transfers between devices  130 us (13%)
  blocking collectives  46.6 us (5%)
  other arithmetic  31.5 us (3%)
  between operations  16.1 us (2%)
    ppermute x14, waiting for transfers between devices, from_behind(): return lax.ppermute(x, axis, pairs)  364 us
    ppermute x14, starting transfers between devices, from_behind(): return lax.ppermute(x, axis, pairs)  130 us
    psum x1, blocking collectives, body(): prompt_share = lax.psum(prompt_share, 'resp')  46.6 us
    unnamed x24, local copies, waits for them, and re-layouts  46.3 us
    all_gather x1, waiting for transfers between devices, body(): lax.all_gather(prompt_values, 'seq', axis=1, tiled=True)  42 us
    sub x8, matrix products, head_pass(): weights = jnp.exp(scores - top_score)  37.7 us
    dot_general x8, matrix products, head_pass(): jnp.einsum('gqk,qgd->kd', probs_low, grad_head, preferred_element_type=jn...  33.4 us
    dot_general x8, matrix products, head_pass(): jnp.einsum('gqk,kd->qgd', probs_low, value_head, preferred_element_type=j...  29.9 us
  transfers between devices with their start and end apart: 17, of which 12 were waited for; matrix products, arithmetic and copies ran while one was open for 7% of the time, Pallas kernels for 0%

commit v1 on v0

v1 whole, which is shorter than its diff:
```python
import math

import jax
import jax.numpy as jnp
from jax import lax
from jax.experimental import pallas as pl
from jax.experimental.pallas import tpu as pltpu
from jax.sharding import PartitionSpec as P

F32 = jnp.float32
BF16 = jnp.bfloat16
HD = 128
SPAN = 128
SCALING = 1.0 / math.sqrt(HD)
SCALING2 = SCALING * math.log2(math.e)
MESH = pl.DeviceIdType.MESH

NT = (((1,), (1,)), ((), ()))
NN = (((1,), (0,)), ((), ()))
TN = (((0,), (0,)), ((), ()))


def dot(a, b, dims):
    return lax.dot_general(a, b, dims, preferred_element_type=F32)


def head_pass(h, valid, qb, db, kv, gacc, ob, qgb, s_scr, d_scr):
    row = lax.broadcasted_iota(jnp.int32, (256, 256), 0)
    col = lax.broadcasted_iota(jnp.int32, (256, 256), 1)
    keep = row <= col
    for g in range(4):
        lanes = slice(g * HD, (g + 1) * HD)
        slot = g % 2
        qg = qb[h, :, :, lanes].reshape(256, HD)
        dog = db[h, :, :, lanes].reshape(256, HD)
        top = None
        for j in range(8):
            s = dot(kv[h, j, 0], qg, NT) * SCALING2
            if j == 4:
                s = jnp.where(keep, s, -jnp.inf)
            s_scr[slot, j] = s
            top_j = jnp.max(s, axis=0, keepdims=True)
            if j > 4:
                top_j = jnp.where(valid[j - 4], top_j, -jnp.inf)
            top = top_j if top is None else jnp.maximum(top, top_j)
        total = None
        centre = None
        for j in range(8):
            shift = top if j <= 4 else jnp.where(valid[j - 4], top, jnp.inf)
            w = jnp.exp2(s_scr[slot, j] - shift)
            dp = dot(kv[h, j, 1], dog, NT)
            s_scr[slot, j] = w
            d_scr[slot, j] = dp
            total_j = jnp.sum(w, axis=0, keepdims=True)
            centre_j = jnp.sum(w * dp, axis=0, keepdims=True)
            total = total_j if total is None else total + total_j
            centre = centre_j if centre is None else centre + centre_j
        inv = 1.0 / total
        centre = centre * inv
        out_t = None
        qgrad_t = None
        for j in range(8):
            probs = s_scr[slot, j] * inv
            score_grad = (probs * (d_scr[slot, j] - centre)).astype(BF16)
            probs_low = probs.astype(BF16)
            dv = dot(probs_low, dog, NN)
            dk = dot(score_grad, qg, NN)
            if g == 0:
                gacc[j, 1] = dv
                gacc[j, 0] = dk
            else:
                gacc[j, 1] += dv
                gacc[j, 0] += dk
            out_j = dot(kv[h, j, 1], probs_low, TN)
            qgrad_j = dot(kv[h, j, 0], score_grad, TN)
            out_t = out_j if out_t is None else out_t + out_j
            qgrad_t = qgrad_j if qgrad_t is None else qgrad_t + qgrad_j
        ob[h, :, :, lanes] = out_t.T.astype(BF16).reshape(2, SPAN, HD)
        qgb[h, :, :, lanes] = (qgrad_t * SCALING).T.astype(BF16).reshape(2, SPAN, HD)


def kernel(
    rp_ref, q_ref, do_ref, rk_ref, rv_ref, pk_ref, pv_ref,
    o_ref, qg_ref, rkg_ref, rvg_ref, pkg_ref, pvg_ref,
    qb, db, kv, relay, sel, gacc, st, sr, ob, qgb, ar, zs, zr, fo, gr, racc, s_scr, d_scr,
    r_z, r_p, r_kv, r_q, r_d, r_o, r_qg, r_g, r_a, r_zz, r_f,
    s_z, s_p, s_kv, s_q, s_d, s_o, s_qg, s_g, s_a, s_zz, s_f,
):
    seq = lax.axis_index("seq")
    resp = lax.axis_index("resp")
    x_lo = seq // 16
    z = (seq // 2) % 8
    core = seq % 2
    chip = z % 4
    z_hi = z // 4
    plane = resp * 2 + x_lo
    head_core = resp // 4
    own_half = core == head_core

    def seq_of(x, zz, k):
        return x * 16 + zz * 2 + k

    def device(s, r):
        return {"seq": s, "resp": r}

    def remote(src, dst, send, recv, s, r):
        return pltpu.make_async_remote_copy(
            src_ref=src, dst_ref=dst, send_sem=send, recv_sem=recv,
            device_id=device(s, r), device_id_type=MESH,
        )

    def wait_for(ref, sem):
        pltpu.make_async_copy(ref, ref, sem).wait()

    def cols(start, width):
        return pl.ds(pl.multiple_of(start, 128), width)

    barrier = pltpu.get_barrier_semaphore()

    def greet(s, r):
        pl.semaphore_signal(barrier, inc=1, device_id=device(s, r), device_id_type=MESH)

    place = resp * 4 + x_lo * 2 + core

    def greet_plane(t, _):
        other = (place + t) % 32
        greet(seq_of((other // 2) % 2, z, other % 2), other // 4)
        return 0

    lax.fori_loop(1, 32, greet_plane, 0)

    def greet_line(t, _):
        greet(seq_of(x_lo, (z + t) % 8, core), resp)
        return 0

    lax.fori_loop(1, 8, greet_line, 0)

    def greet_group(t, _):
        greet(seq_of(x_lo, z_hi * 4 + (chip + t) % 4, 1 - core), resp)
        return 0

    lax.fori_loop(1, 4, greet_group, 0)

    for d in range(1, 4):

        @pl.when(chip < d)
        def _():
            for h in range(4):
                kv[h, 4 + d] = jnp.zeros((2, 256, HD), BF16)

    pl.semaphore_wait(barrier, 41)

    mine = cols(resp * HD, HD)
    for which, src in enumerate((pk_ref, pv_ref)):
        pltpu.make_async_copy(src.at[:, :, mine], relay.at[which, :, z], r_z).start()

        def send_line(t, _, which=which, src=src):
            remote(
                src.at[:, :, mine], relay.at[which, :, z], s_z, r_z,
                seq_of(x_lo, (z + t) % 8, core), resp,
            ).start()
            return 0

        lax.fori_loop(1, 8, send_line, 0)

    def rotated(step):
        return (step + resp) % 4

    def send_inputs(step):
        h = rotated(step)
        own = cols((core * 4 + h) * 512, 512)
        other = cols(((1 - core) * 4 + h) * 512, 512)
        sibling = seq_of(x_lo, z, 1 - core)
        for src, dst, send, recv in ((q_ref, qb, s_q, r_q), (do_ref, db, s_d, r_d)):
            remote(src.at[:, other], dst.at[h, core], send, recv.at[h], sibling, resp).start()
            pltpu.make_async_copy(src.at[:, own], dst.at[h, core], recv.at[h]).start()
        rows = pl.ds(pl.multiple_of(core * SPAN, SPAN), SPAN)
        for which, src in enumerate((rk_ref, rv_ref)):
            own = cols((core * 4 + h) * HD, HD)
            other = cols(((1 - core) * 4 + h) * HD, HD)
            dst = kv.at[h, 4, which, rows]
            pltpu.make_async_copy(src.at[:, own], dst, r_kv.at[h, 0]).start()
            remote(src.at[:, other], dst, s_kv.at[0], r_kv.at[h, 0], sibling, resp).start()
        for d in range(1, 4):

            @pl.when(chip + d <= 3)
            def _():
                for k in range(2):
                    for which, src in enumerate((rk_ref, rv_ref)):
                        remote(
                            src.at[:, cols((k * 4 + h) * HD, HD)],
                            kv.at[h, 4 + d, which, rows],
                            s_kv.at[d], r_kv.at[h, d],
                            seq_of(x_lo, z + d, k), resp,
                        ).start()

    send_inputs(0)

    wait_for(relay, r_z)
    quarter = x_lo * 2 + core

    def send_plane(step, _):
        for hi in range(2):
            for xl in range(2):
                r = (resp + 4 - step) % 4 + 4 * ((resp // 4 + hi) % 2)
                x = (x_lo + xl) % 2
                second = rp_ref[r * 4 + x * 2 + z_hi] == 1
                at = step * 4 + hi * 2 + xl
                for which in range(2):
                    sel[at, which] = jnp.where(
                        second, relay[which, 1].reshape(256, HD), relay[which, 0].reshape(256, HD)
                    )
                dst = kv.at[resp % 4, quarter]
                recv = r_p.at[resp % 4]
                here = (at == 0) & own_half

                @pl.when(here)
                def _():
                    pltpu.make_async_copy(sel.at[at], dst, recv).start()

                @pl.when(jnp.logical_not(here))
                def _():
                    remote(
                        sel.at[at], dst, s_p.at[at], recv, seq_of(x, z, head_core), r
                    ).start()

        return 0

    lax.fori_loop(0, 4, send_plane, 0)
    for step in range(1, 4):
        send_inputs(step)

    valid = [chip >= d for d in range(4)]

    def run_head(step, _):
        h = rotated(step)
        wait_for(qb.at[h], r_q.at[h])
        wait_for(db.at[h], r_d.at[h])
        for d in range(4):

            @pl.when(chip >= d)
            def _():
                wait_for(kv.at[h, 4 + d], r_kv.at[h, d])

        wait_for(kv.at[h, pl.ds(0, 4)], r_p.at[h])
        head_pass(h, valid, qb, db, kv, gacc, ob, qgb, s_scr, d_scr)
        for j in range(4):
            st[h, j, 0] = (gacc[j, 0] * SCALING).astype(BF16)
            st[h, j, 1] = gacc[j, 1].astype(BF16)
        head = core * 4 + h
        for x in range(2):
            for k in range(2):
                here = (head == resp) & (x == x_lo) & (k == core)
                src = st.at[h, x * 2 + k]

                @pl.when(here)
                def _():
                    pltpu.make_async_copy(src, ar.at[plane], r_a).start()

                @pl.when(jnp.logical_not(here))
                def _():
                    remote(
                        src, ar.at[plane], s_a.at[h, x * 2 + k], r_a, seq_of(x, z, k), head
                    ).start()

        for d in range(4):

            @pl.when(chip >= d)
            def _():
                for k in range(2):
                    rows = slice(k * SPAN, (k + 1) * SPAN)
                    sr[h, d, k, 0] = (gacc[4 + d, 0, rows] * SCALING).astype(BF16)
                    sr[h, d, k, 1] = gacc[4 + d, 1, rows].astype(BF16)
                if d == 0:
                    dst = gr.at[0, head]
                    pltpu.make_async_copy(sr.at[h, 0, core], dst, r_g.at[0]).start()
                    remote(
                        sr.at[h, 0, 1 - core], dst, s_g.at[0], r_g.at[0],
                        seq_of(x_lo, z, 1 - core), resp,
                    ).start()
                else:
                    for k in range(2):
                        remote(
                            sr.at[h, d, k], gr.at[d, head], s_g.at[d], r_g.at[d],
                            seq_of(x_lo, z - d, k), resp,
                        ).start()

        where = cols(head * 512, 512)
        for src, dst, send, recv in ((ob, o_ref, s_o, r_o), (qgb, qg_ref, s_qg, r_qg)):
            pltpu.make_async_copy(src.at[h, core], dst.at[:, where], recv).start()
            remote(
                src.at[h, 1 - core], dst.at[:, where], send, recv,
                seq_of(x_lo, z, 1 - core), resp,
            ).start()
        return 0

    lax.fori_loop(0, 4, run_head, 0)

    wait_for(ar, r_a)
    second = [rp_ref[(a // 2) * 4 + (a % 2) * 2 + z_hi] == 1 for a in range(16)]

    def sum_plane(t, _):
        to = (z + t) % 8
        rows = pl.ds(pl.multiple_of(to * 32, 32), 32)
        for which in range(2):
            sums = [jnp.zeros((32, HD), F32), jnp.zeros((32, HD), F32)]
            for a in range(16):
                term = ar[a, which, rows].astype(F32)
                sums[0] += jnp.where(second[a], 0.0, term)
                sums[1] += jnp.where(second[a], term, 0.0)
            for p in range(2):
                zs[to, p, which] = sums[p].astype(BF16)

        @pl.when(t == 0)
        def _():
            pltpu.make_async_copy(zs.at[to], zr.at[z], r_zz).start()

        @pl.when(t > 0)
        def _():
            remote(
                zs.at[to], zr.at[z], s_zz, r_zz, seq_of(x_lo, to, core), resp
            ).start()

        return 0

    lax.fori_loop(0, 8, sum_plane, 0)

    wait_for(gr.at[0], r_g.at[0])
    racc[...] = gr[0].astype(F32)
    for d in range(1, 4):

        @pl.when(chip + d <= 3)
        def _():
            wait_for(gr.at[d], r_g.at[d])
            racc[...] += gr[d].astype(F32)

    for n in range(8):
        rkg_ref[:, n * HD : (n + 1) * HD] = racc[n, 0].astype(BF16)
        rvg_ref[:, n * HD : (n + 1) * HD] = racc[n, 1].astype(BF16)

    wait_for(zr, r_zz)
    for which in range(2):
        for p in range(2):
            final = zr[0, p, which].astype(F32)
            for n in range(1, 8):
                final = final + zr[n, p, which].astype(F32)
            fo[which, p] = final.astype(BF16)
    for which, dst in enumerate((pkg_ref, pvg_ref)):
        pltpu.make_async_copy(fo.at[which], dst.at[:, :, mine], r_f.at[which]).start()

        def send_replica(t, _, which=which, dst=dst):
            remote(
                fo.at[which], dst.at[:, :, mine], s_f.at[which], r_f.at[which],
                seq, (resp + t) % 8,
            ).start()
            return 0

        lax.fori_loop(1, 8, send_replica, 0)

    wait_for(o_ref, r_o)
    wait_for(qg_ref, r_qg)
    wait_for(pkg_ref, r_f.at[0])
    wait_for(pvg_ref, r_f.at[1])

    wait_for(relay.at[:, :, pl.ds(0, 7)], s_z)
    for at in range(16):
        if at == 0:

            @pl.when(jnp.logical_not(own_half))
            def _():
                wait_for(sel.at[0], s_p.at[0])
        else:
            wait_for(sel.at[at], s_p.at[at])
    wait_for(kv.at[0, pl.ds(0, 2)], s_kv.at[0])
    wait_for(gr.at[0, pl.ds(0, 4)], s_g.at[0])
    for d in range(1, 4):

        @pl.when(chip + d <= 3)
        def _():
            wait_for(kv.at[0, pl.ds(0, 4)], s_kv.at[d])

        @pl.when(chip >= d)
        def _():
            wait_for(gr.at[0], s_g.at[d])

    wait_for(qb.at[:, 0], s_q)
    wait_for(db.at[:, 0], s_d)
    wait_for(ob.at[:, 0], s_o)
    wait_for(qgb.at[:, 0], s_qg)
    for h in range(4):
        for n in range(4):
            here = (core * 4 + h == resp) & (n == quarter)

            @pl.when(jnp.logical_not(here))
            def _():
                wait_for(st.at[h, n], s_a.at[h, n])

    wait_for(zr.at[pl.ds(0, 7)], s_zz)
    for which in range(2):
        wait_for(zr.at[pl.ds(0, 7), 0], s_f.at[which])


def body(queries, resp_keys, resp_values, prompt_keys, prompt_values, response_prompt, out_grad):
    anywhere = pl.BlockSpec(memory_space=pl.ANY)
    vmem = pl.BlockSpec(memory_space=pltpu.VMEM)
    dma = pltpu.SemaphoreType.DMA
    rows = jax.ShapeDtypeStruct((SPAN, 4096), BF16)
    block = jax.ShapeDtypeStruct((SPAN, 1024), BF16)
    shard = jax.ShapeDtypeStruct((2, 32, 1024), BF16)
    attended, query_grad, rkg, rvg, pkg, pvg = pl.pallas_call(
        kernel,
        out_shape=(rows, rows, block, block, shard, shard),
        in_specs=[pl.BlockSpec(memory_space=pltpu.SMEM)] + [anywhere] * 6,
        out_specs=(anywhere, anywhere, vmem, vmem, anywhere, anywhere),
        scratch_shapes=[
            pltpu.VMEM((4, 2, SPAN, 512), BF16),
            pltpu.VMEM((4, 2, SPAN, 512), BF16),
            pltpu.VMEM((4, 8, 2, 256, HD), BF16),
            pltpu.VMEM((2, 2, 8, 32, HD), BF16),
            pltpu.VMEM((16, 2, 256, HD), BF16),
            pltpu.VMEM((8, 2, 256, HD), F32),
            pltpu.VMEM((4, 4, 2, 256, HD), BF16),
            pltpu.VMEM((4, 4, 2, 2, SPAN, HD), BF16),
            pltpu.VMEM((4, 2, SPAN, 512), BF16),
            pltpu.VMEM((4, 2, SPAN, 512), BF16),
            pltpu.VMEM((16, 2, 256, HD), BF16),
            pltpu.VMEM((8, 2, 2, 32, HD), BF16),
            pltpu.VMEM((8, 2, 2, 32, HD), BF16),
            pltpu.VMEM((2, 2, 32, HD), BF16),
            pltpu.VMEM((4, 8, 2, SPAN, HD), BF16),
            pltpu.VMEM((8, 2, SPAN, HD), F32),
            pltpu.VMEM((2, 8, 256, 256), F32),
            pltpu.VMEM((2, 8, 256, 256), F32),
            dma(()),
            dma((4,)),
            dma((4, 4)),
            dma((4,)),
            dma((4,)),
            dma(()),
            dma(()),
            dma((4,)),
            dma(()),
            dma(()),
            dma((2,)),
            dma(()),
            dma((16,)),
            dma((4,)),
            dma(()),
            dma(()),
            dma(()),
            dma(()),
            dma((4,)),
            dma((4, 4)),
            dma(()),
            dma((2,)),
        ],
        compiler_params=pltpu.CompilerParams(
            collective_id=0, has_side_effects=True, vmem_limit_bytes=56 * 1024 * 1024
        ),
        name="attention_step",
    )(
        response_prompt, queries[0], out_grad[0], resp_keys[0], resp_values[0],
        prompt_keys, prompt_values,
    )
    return (attended[None], query_grad[None], rkg[None], rvg[None], pkg, pvg)


def solution(mesh):
    by_row = P("resp", "seq", None)
    shared = P(None, "seq", None)
    return jax.shard_map(
        body,
        mesh=mesh,
        in_specs=(by_row, by_row, by_row, shared, shared, P(), by_row),
        out_specs=(by_row, by_row, by_row, by_row, shared, shared),
        check_vma=False,
    )
```

time: 966 us -> 115 us (0.12)
  waiting for transfers between devices: 434 us -> 0 us
  matrix products: 159 us -> 0 us
  local copies, waits for them, and re-layouts: 140 us -> 7.12 us
  starting transfers between devices: 130 us -> 0 us
  Pallas kernels: 0 us -> 107 us
  blocking collectives: 46.6 us -> 0 us
  other arithmetic: 31.5 us -> 0 us
  between operations: 16.1 us -> 0.66 us
    ppermute x14 -> x0, waiting for transfers between devices: 364 us -> none  [from_behind(): return lax.ppermute(x, axis, pairs)]
    ppermute x14 -> x0, starting transfers between devices: 130 us -> none  [from_behind(): return lax.ppermute(x, axis, pairs)]
    dot_general x40 -> x0, matrix products: 121 us -> none  [the longest x8 33.4 us: head_pass(): jnp.einsum('gqk,qgd->kd', probs_low, grad_head, preferred_element_type=jn...]
    pallas_call x0 -> x1, Pallas kernels: none -> 107 us  [body(): pl.pallas_call(kernel, out_shape=(rows, rows, block, block, shard, shard)...]
    psum x1 -> x0, blocking collectives: 46.6 us -> none  [body(): prompt_share = lax.psum(prompt_share, 'resp')]
    all_gather x2 -> x0, waiting for transfers between devices: 42 us -> none  [the longest x1 42 us: body(): lax.all_gather(prompt_values, 'seq', axis=1, tiled=True)]
    unnamed x24 -> x16, local copies, waits for them, and re-layouts: 46.3 us -> 7.12 us
    sub x8 -> x0, matrix products: 37.7 us -> none  [head_pass(): weights = jnp.exp(scores - top_score)]
  transfers between devices with their start and end apart: 17 -> 0, of which waited for: 12 -> 0; matrix products, arithmetic and copies ran while one was open for 7% -> 0% of each run, Pallas kernels for 0% -> 0%
where the time goes in v1:
time: 115 us
  Pallas kernels  107 us (93%)
  local copies, waits for them, and re-layouts  7.12 us (6%)
    pallas_call x1, Pallas kernels, body(): pl.pallas_call(kernel, out_shape=(rows, rows, block, block, shard, shard)...  107 us
    unnamed x16, local copies, waits for them, and re-layouts  7.12 us

profile of v1, /device:TPU:6, one launch (start us, length us, event | category | flops | bytes accessed | tf_op | source)
XLA Modules:
  0.0 115.3 jit_solution(3857795590300794394)
XLA Ops:
  0.6 107.5 %attention_step.1 = (bf16[128,4096]{1,0:T(8,128)(2,1)}, bf16[128,4096]{1,0:T(8,128)(2,1)}, bf16[128,1024]{1,0:T(8,128)(2,1)}, bf16[128,1024]{1,0:T(8,128)(2,1)},...) custom-call(s32[32]{0:T(128)} %rp_ref.1, bf16[128,4096]{1,0:T(8,128)(2,1)} %bitcast.8, ...), custom_call_target="tpu_custom_call" | custom-call | tf_op jit(solution)/shard_map/attention_step/pallas_call | solution.py:410
  108.1 0.0 copy-start
  108.1 2.4 %copy.19 = bf16[1,128,4096]{2,1,0:T(8,128)(2,1)} copy(bf16[1,128,4096]{2,1,0:T(8,128)(2,1)} %bitcast.11) | data formatting | bytes 2097152
  110.5 0.0 copy-done
  110.5 0.0 copy-start.2
  110.5 1.0 copy.20
  111.5 0.1 copy-done.2
  111.6 0.0 copy-start.1
  111.6 0.7 copy.21
  112.3 0.3 copy-done.1
  112.7 0.0 copy-start.4
  112.7 0.7 copy.22
  113.4 0.3 copy-done.4
  113.7 0.0 copy-start.3
  113.7 0.7 copy.23
  114.3 0.3 copy-done.3
  114.6 0.7 copy.24
Async XLA Ops:
  108.1 2.4 %copy-start = (bf16[128,4096]{1,0:T(8,128)(2,1)S(1)}, bf16[128,4096]{1,0:T(8,128)(2,1)}, u32[]{:S(2)}) copy-start(bf16[128,4096]{1,0:T(8,128)(2,1)} %get-tuple-element.13) | copy-start | bytes 3145732
  110.5 1.1 copy-start.2
  111.6 1.0 copy-start.1
  112.7 1.0 copy-start.4
  113.7 1.0 copy-start.3

commit v2 on v1

--- a/solution.py
+++ b/solution.py
@@ -24,7 +24,7 @@
     return lax.dot_general(a, b, dims, preferred_element_type=F32)
 
 
-def head_pass(h, valid, qb, db, kv, gacc, ob, qgb, s_scr, d_scr):
+def head_pass(h, valid, between, qb, db, kv, gacc, ob, qgb, s_scr, d_scr):
     row = lax.broadcasted_iota(jnp.int32, (256, 256), 0)
     col = lax.broadcasted_iota(jnp.int32, (256, 256), 1)
     keep = row <= col
@@ -77,14 +77,15 @@
             qgrad_t = qgrad_j if qgrad_t is None else qgrad_t + qgrad_j
         ob[h, :, :, lanes] = out_t.T.astype(BF16).reshape(2, SPAN, HD)
         qgb[h, :, :, lanes] = (qgrad_t * SCALING).T.astype(BF16).reshape(2, SPAN, HD)
+        between(g)
 
 
 def kernel(
     rp_ref, q_ref, do_ref, rk_ref, rv_ref, pk_ref, pv_ref,
     o_ref, qg_ref, rkg_ref, rvg_ref, pkg_ref, pvg_ref,
-    qb, db, kv, relay, sel, gacc, st, sr, ob, qgb, ar, zs, zr, fo, gr, racc, s_scr, d_scr,
-    r_z, r_p, r_kv, r_q, r_d, r_o, r_qg, r_g, r_a, r_zz, r_f,
-    s_z, s_p, s_kv, s_q, s_d, s_o, s_qg, s_g, s_a, s_zz, s_f,
+    qb, db, kv, stage, relay, sel, gacc, st, sr, ob, qgb, ar, zs, zr, fo, fr, gr, mb, racc, s_scr, d_scr,
+    r_s, r_z, r_p, r_kv, r_q, r_d, r_o, r_qg, r_g, r_m, r_a, r_zz, r_f,
+    s_z, s_p, s_kv, s_w, s_q, s_d, s_o, s_qg, s_g, s_a, s_zz, s_f,
 ):
     seq = lax.axis_index("seq")
     resp = lax.axis_index("resp")
@@ -115,6 +116,10 @@
     def cols(start, width):
         return pl.ds(pl.multiple_of(start, 128), width)
 
+    mine = cols(resp * HD, HD)
+    for which, src in enumerate((pk_ref, pv_ref)):
+        pltpu.make_async_copy(src.at[:, :, mine], stage.at[which], r_s).start()
+
     barrier = pltpu.get_barrier_semaphore()
 
     def greet(s, r):
@@ -150,65 +155,106 @@
 
     pl.semaphore_wait(barrier, 41)
 
-    mine = cols(resp * HD, HD)
-    for which, src in enumerate((pk_ref, pv_ref)):
-        pltpu.make_async_copy(src.at[:, :, mine], relay.at[which, :, z], r_z).start()
-
-        def send_line(t, _, which=which, src=src):
-            remote(
-                src.at[:, :, mine], relay.at[which, :, z], s_z, r_z,
-                seq_of(x_lo, (z + t) % 8, core), resp,
-            ).start()
-            return 0
-
-        lax.fori_loop(1, 8, send_line, 0)
-
-    def rotated(step):
-        return (step + resp) % 4
+    wait_for(stage, r_s)
+    pltpu.make_async_copy(stage, relay.at[z], r_z).start()
+
+    def send_line(t, _):
+        remote(stage, relay.at[z], s_z, r_z, seq_of(x_lo, (z + t) % 8, core), resp).start()
+        return 0
+
+    lax.fori_loop(1, 8, send_line, 0)
+
+    y = resp // 2
+    x_hi = resp % 2
+
+    def head_at(step, k):
+        odd = (y + step // 2) % 2
+        away = ((y - 2 * k - odd + 4) % 4) // 2
+        return odd * 2 + (x_hi + step + away) % 2
 
     def send_inputs(step):
-        h = rotated(step)
+        h = head_at(step, core)
+        h_other = head_at(step, 1 - core)
         own = cols((core * 4 + h) * 512, 512)
-        other = cols(((1 - core) * 4 + h) * 512, 512)
+        other = cols(((1 - core) * 4 + h_other) * 512, 512)
         sibling = seq_of(x_lo, z, 1 - core)
         for src, dst, send, recv in ((q_ref, qb, s_q, r_q), (do_ref, db, s_d, r_d)):
-            remote(src.at[:, other], dst.at[h, core], send, recv.at[h], sibling, resp).start()
+            remote(
+                src.at[:, other], dst.at[h_other, core], send, recv.at[h_other], sibling, resp
+            ).start()
             pltpu.make_async_copy(src.at[:, own], dst.at[h, core], recv.at[h]).start()
         rows = pl.ds(pl.multiple_of(core * SPAN, SPAN), SPAN)
         for which, src in enumerate((rk_ref, rv_ref)):
             own = cols((core * 4 + h) * HD, HD)
-            other = cols(((1 - core) * 4 + h) * HD, HD)
-            dst = kv.at[h, 4, which, rows]
-            pltpu.make_async_copy(src.at[:, own], dst, r_kv.at[h, 0]).start()
-            remote(src.at[:, other], dst, s_kv.at[0], r_kv.at[h, 0], sibling, resp).start()
-        for d in range(1, 4):
-
-            @pl.when(chip + d <= 3)
-            def _():
-                for k in range(2):
-                    for which, src in enumerate((rk_ref, rv_ref)):
-                        remote(
-                            src.at[:, cols((k * 4 + h) * HD, HD)],
-                            kv.at[h, 4 + d, which, rows],
-                            s_kv.at[d], r_kv.at[h, d],
-                            seq_of(x_lo, z + d, k), resp,
-                        ).start()
+            other = cols(((1 - core) * 4 + h_other) * HD, HD)
+            pltpu.make_async_copy(
+                src.at[:, own], kv.at[h, 4, which, rows], r_kv.at[h, 0]
+            ).start()
+            remote(
+                src.at[:, other], kv.at[h_other, 4, which, rows],
+                s_kv.at[0], r_kv.at[h_other, 0], sibling, resp,
+            ).start()
+        send_keys(step, 1)
+
+    def sends_to(d):
+        return (chip + d <= 3) if d != 2 else (chip == 0)
+
+    def send_keys(step, d):
+        rows = pl.ds(pl.multiple_of(core * SPAN, SPAN), SPAN)
+
+        @pl.when(sends_to(d))
+        def _():
+            for k in range(2):
+                to = head_at(step, k)
+                for which, src in enumerate((rk_ref, rv_ref)):
+                    remote(
+                        src.at[:, cols((k * 4 + to) * HD, HD)],
+                        kv.at[to, 4 + d, which, rows],
+                        s_kv.at[d], r_kv.at[to, d],
+                        seq_of(x_lo, z + d, k), resp,
+                    ).start()
+
+    def hand_on(step):
+        h = head_at(step, core)
+
+        @pl.when(chip == 2)
+        def _():
+            wait_for(kv.at[h, 5], r_kv.at[h, 1])
+            remote(
+                kv.at[h, 5], kv.at[h, 6], s_w, r_kv.at[h, 2], seq_of(x_lo, z + 1, core), resp
+            ).start()
+
+    def merge(step):
+        h = head_at(step, core)
+
+        @pl.when(chip == 2)
+        def _():
+            wait_for(mb.at[h], r_m.at[h])
+            sr[h, 1] = (sr[h, 1].astype(F32) + mb[h].astype(F32)).astype(BF16)
+            for k in range(2):
+                remote(
+                    sr.at[h, 1, k], gr.at[1, core * 4 + h], s_g.at[1], r_g.at[1],
+                    seq_of(x_lo, z - 1, k), resp,
+                ).start()
 
     send_inputs(0)
 
     wait_for(relay, r_z)
     quarter = x_lo * 2 + core
 
-    def send_plane(step, _):
+    def send_plane(step):
+        shift = 2 * (step % 2) + step // 2
         for hi in range(2):
             for xl in range(2):
-                r = (resp + 4 - step) % 4 + 4 * ((resp // 4 + hi) % 2)
+                r = ((y + shift + 2 * hi) % 4) * 2 + (x_hi + hi) % 2
                 x = (x_lo + xl) % 2
                 second = rp_ref[r * 4 + x * 2 + z_hi] == 1
                 at = step * 4 + hi * 2 + xl
                 for which in range(2):
                     sel[at, which] = jnp.where(
-                        second, relay[which, 1].reshape(256, HD), relay[which, 0].reshape(256, HD)
+                        second,
+                        relay[:, which, 1].reshape(256, HD),
+                        relay[:, which, 0].reshape(256, HD),
                     )
                 dst = kv.at[resp % 4, quarter]
                 recv = r_p.at[resp % 4]
@@ -224,26 +270,56 @@
                         sel.at[at], dst, s_p.at[at], recv, seq_of(x, z, head_core), r
                     ).start()
 
-        return 0
-
-    lax.fori_loop(0, 4, send_plane, 0)
-    for step in range(1, 4):
-        send_inputs(step)
+    send_plane(0)
+    send_keys(0, 2)
+    send_keys(0, 3)
+    hand_on(0)
 
     valid = [chip >= d for d in range(4)]
 
     def run_head(step, _):
-        h = rotated(step)
+        h = head_at(step, core)
         wait_for(qb.at[h], r_q.at[h])
         wait_for(db.at[h], r_d.at[h])
         for d in range(4):
 
-            @pl.when(chip >= d)
+            @pl.when((chip >= d) if d != 1 else (chip % 2 == 1))
             def _():
                 wait_for(kv.at[h, 4 + d], r_kv.at[h, d])
 
         wait_for(kv.at[h, pl.ds(0, 4)], r_p.at[h])
-        head_pass(h, valid, qb, db, kv, gacc, ob, qgb, s_scr, d_scr)
+
+        @pl.when(step == 0)
+        def _():
+            send_plane(1)
+            send_inputs(1)
+
+        def between(g):
+            if g == 0:
+
+                @pl.when(step == 0)
+                def _():
+                    send_keys(1, 2)
+                    send_keys(1, 3)
+            elif g == 1:
+
+                @pl.when(step < 3)
+                def _():
+                    hand_on(step + 1)
+            elif g == 2:
+
+                @pl.when(step < 2)
+                def _():
+                    send_plane(step + 2)
+                    send_inputs(step + 2)
+                    send_keys(step + 2, 2)
+                    send_keys(step + 2, 3)
+
+                @pl.when(step > 0)
+                def _():
+                    merge(step - 1)
+
+        head_pass(h, valid, between, qb, db, kv, gacc, ob, qgb, s_scr, d_scr)
         for j in range(4):
             st[h, j, 0] = (gacc[j, 0] * SCALING).astype(BF16)
             st[h, j, 1] = gacc[j, 1].astype(BF16)
@@ -262,6 +338,13 @@
                     remote(
                         src, ar.at[plane], s_a.at[h, x * 2 + k], r_a, seq_of(x, z, k), head
                     ).start()
+
+        def send_terms(d):
+            for k in range(2):
+                remote(
+                    sr.at[h, d, k], gr.at[d, head], s_g.at[d], r_g.at[d],
+                    seq_of(x_lo, z - d, k), resp,
+                ).start()
 
         for d in range(4):
 
@@ -278,12 +361,25 @@
                         sr.at[h, 0, 1 - core], dst, s_g.at[0], r_g.at[0],
                         seq_of(x_lo, z, 1 - core), resp,
                     ).start()
+                elif d == 1:
+
+                    @pl.when(chip != 2)
+                    def _():
+                        send_terms(d)
+                elif d == 2:
+
+                    @pl.when(chip == 2)
+                    def _():
+                        send_terms(d)
+
+                    @pl.when(chip == 3)
+                    def _():
+                        remote(
+                            sr.at[h, 2], mb.at[h], s_g.at[2], r_m.at[h],
+                            seq_of(x_lo, z - 1, core), resp,
+                        ).start()
                 else:
-                    for k in range(2):
-                        remote(
-                            sr.at[h, d, k], gr.at[d, head], s_g.at[d], r_g.at[d],
-                            seq_of(x_lo, z - d, k), resp,
-                        ).start()
+                    send_terms(d)
 
         where = cols(head * 512, 512)
         for src, dst, send, recv in ((ob, o_ref, s_o, r_o), (qgb, qg_ref, s_qg, r_qg)):
@@ -295,6 +391,8 @@
         return 0
 
     lax.fori_loop(0, 4, run_head, 0)
+
+    merge(3)
 
     wait_for(ar, r_a)
     second = [rp_ref[(a // 2) * 4 + (a % 2) * 2 + z_hi] == 1 for a in range(16)]
@@ -329,7 +427,7 @@
     racc[...] = gr[0].astype(F32)
     for d in range(1, 4):
 
-        @pl.when(chip + d <= 3)
+        @pl.when(sends_to(d))
         def _():
             wait_for(gr.at[d], r_g.at[d])
             racc[...] += gr[d].astype(F32)
@@ -345,24 +443,22 @@
             for n in range(1, 8):
                 final = final + zr[n, p, which].astype(F32)
             fo[which, p] = final.astype(BF16)
-    for which, dst in enumerate((pkg_ref, pvg_ref)):
-        pltpu.make_async_copy(fo.at[which], dst.at[:, :, mine], r_f.at[which]).start()
-
-        def send_replica(t, _, which=which, dst=dst):
-            remote(
-                fo.at[which], dst.at[:, :, mine], s_f.at[which], r_f.at[which],
-                seq, (resp + t) % 8,
-            ).start()
-            return 0
-
-        lax.fori_loop(1, 8, send_replica, 0)
+    pltpu.make_async_copy(fo, fr.at[resp], r_f).start()
+
+    def send_replica(t, _):
+        remote(fo, fr.at[resp], s_f, r_f, seq, (resp + t) % 8).start()
+        return 0
+
+    lax.fori_loop(1, 8, send_replica, 0)
 
     wait_for(o_ref, r_o)
     wait_for(qg_ref, r_qg)
-    wait_for(pkg_ref, r_f.at[0])
-    wait_for(pvg_ref, r_f.at[1])
-
-    wait_for(relay.at[:, :, pl.ds(0, 7)], s_z)
+    wait_for(fr, r_f)
+    for n in range(8):
+        pkg_ref[:, :, n * HD : (n + 1) * HD] = fr[n, 0]
+        pvg_ref[:, :, n * HD : (n + 1) * HD] = fr[n, 1]
+
+    wait_for(relay.at[pl.ds(0, 7)], s_z)
     for at in range(16):
         if at == 0:
 
@@ -375,13 +471,17 @@
     wait_for(gr.at[0, pl.ds(0, 4)], s_g.at[0])
     for d in range(1, 4):
 
-        @pl.when(chip + d <= 3)
+        @pl.when(sends_to(d))
         def _():
             wait_for(kv.at[0, pl.ds(0, 4)], s_kv.at[d])
 
         @pl.when(chip >= d)
         def _():
             wait_for(gr.at[0], s_g.at[d])
+
+    @pl.when(chip == 2)
+    def _():
+        wait_for(kv.at[0, pl.ds(0, 4)], s_w)
 
     wait_for(qb.at[:, 0], s_q)
     wait_for(db.at[:, 0], s_d)
@@ -396,8 +496,12 @@
                 wait_for(st.at[h, n], s_a.at[h, n])
 
     wait_for(zr.at[pl.ds(0, 7)], s_zz)
-    for which in range(2):
-        wait_for(zr.at[pl.ds(0, 7), 0], s_f.at[which])
+    wait_for(fr.at[pl.ds(0, 7)], s_f)
+
+
+def finish(*refs):
+    for src, dst in zip(refs[:6], refs[6:]):
+        dst[...] = src[...]
 
 
 def body(queries, resp_keys, resp_values, prompt_keys, prompt_values, response_prompt, out_grad):
@@ -407,16 +511,17 @@
     rows = jax.ShapeDtypeStruct((SPAN, 4096), BF16)
     block = jax.ShapeDtypeStruct((SPAN, 1024), BF16)
     shard = jax.ShapeDtypeStruct((2, 32, 1024), BF16)
-    attended, query_grad, rkg, rvg, pkg, pvg = pl.pallas_call(
+    results = pl.pallas_call(
         kernel,
         out_shape=(rows, rows, block, block, shard, shard),
         in_specs=[pl.BlockSpec(memory_space=pltpu.SMEM)] + [anywhere] * 6,
-        out_specs=(anywhere, anywhere, vmem, vmem, anywhere, anywhere),
+        out_specs=(anywhere, anywhere, vmem, vmem, vmem, vmem),
         scratch_shapes=[
             pltpu.VMEM((4, 2, SPAN, 512), BF16),
             pltpu.VMEM((4, 2, SPAN, 512), BF16),
             pltpu.VMEM((4, 8, 2, 256, HD), BF16),
-            pltpu.VMEM((2, 2, 8, 32, HD), BF16),
+            pltpu.VMEM((2, 2, 32, HD), BF16),
+            pltpu.VMEM((8, 2, 2, 32, HD), BF16),
             pltpu.VMEM((16, 2, 256, HD), BF16),
             pltpu.VMEM((8, 2, 256, HD), F32),
             pltpu.VMEM((4, 4, 2, 256, HD), BF16),
@@ -427,10 +532,13 @@
             pltpu.VMEM((8, 2, 2, 32, HD), BF16),
             pltpu.VMEM((8, 2, 2, 32, HD), BF16),
             pltpu.VMEM((2, 2, 32, HD), BF16),
+            pltpu.VMEM((8, 2, 2, 32, HD), BF16),
             pltpu.VMEM((4, 8, 2, SPAN, HD), BF16),
+            pltpu.VMEM((4, 2, 2, SPAN, HD), BF16),
             pltpu.VMEM((8, 2, SPAN, HD), F32),
             pltpu.VMEM((2, 8, 256, 256), F32),
             pltpu.VMEM((2, 8, 256, 256), F32),
+            dma(()),
             dma(()),
             dma((4,)),
             dma((4, 4)),
@@ -439,9 +547,10 @@
             dma(()),
             dma(()),
             dma((4,)),
-            dma(()),
-            dma(()),
-            dma((2,)),
+            dma((4,)),
+            dma(()),
+            dma(()),
+            dma(()),
             dma(()),
             dma((16,)),
             dma((4,)),
@@ -449,10 +558,11 @@
             dma(()),
             dma(()),
             dma(()),
+            dma(()),
             dma((4,)),
             dma((4, 4)),
             dma(()),
-            dma((2,)),
+            dma(()),
         ],
         compiler_params=pltpu.CompilerParams(
             collective_id=0, has_side_effects=True, vmem_limit_bytes=56 * 1024 * 1024
@@ -462,6 +572,19 @@
         response_prompt, queries[0], out_grad[0], resp_keys[0], resp_values[0],
         prompt_keys, prompt_values,
     )
+    parts = (
+        [pl.BlockSpec((SPAN, 1024), lambda i: (0, i))] * 2
+        + [pl.BlockSpec((SPAN, 256), lambda i: (0, i))] * 2
+        + [pl.BlockSpec((2, 32, 256), lambda i: (0, 0, i))] * 2
+    )
+    attended, query_grad, rkg, rvg, pkg, pvg = pl.pallas_call(
+        finish,
+        out_shape=(rows, rows, block, block, shard, shard),
+        grid=(4,),
+        in_specs=parts,
+        out_specs=parts,
+        name="finish",
+    )(*results)
     return (attended[None], query_grad[None], rkg[None], rvg[None], pkg, pvg)
 
 

time: 115 us -> 102 us (0.89); the launches traced: 115 us -> 99.7 us
  Pallas kernels: 107 us -> 99 us
  local copies, waits for them, and re-layouts: 7.12 us -> 0 us
    pallas_call x1, Pallas kernels: 107 us -> 95 us  [body(): pl.pallas_call(kernel, out_shape=(rows, rows, block, block, shard, shard)...]
    unnamed x16 -> x0, local copies, waits for them, and re-layouts: 7.12 us -> none
    pallas_call x0 -> x1, Pallas kernels: none -> 4.03 us  [body(): pl.pallas_call(finish, out_shape=(rows, rows, block, block, shard, shard)...]
where the time goes in v2:
time: 102 us; the launch traced here: 99.7 us
  Pallas kernels  99 us (97%)
    pallas_call x1, Pallas kernels, body(): pl.pallas_call(kernel, out_shape=(rows, rows, block, block, shard, shard)...  95 us
    pallas_call x1, Pallas kernels, body(): pl.pallas_call(finish, out_shape=(rows, rows, block, block, shard, shard)...  4.03 us

profile of v2, /device:TPU:6, one launch (start us, length us, event | category | flops | bytes accessed | tf_op | source)
XLA Modules:
  0.0 99.7 jit_solution(16393843122210202907)
XLA Ops:
  0.6 95.0 %attention_step.1 = (bf16[128,4096]{1,0:T(8,128)(2,1)}, bf16[128,4096]{1,0:T(8,128)(2,1)}, bf16[128,1024]{1,0:T(8,128)(2,1)}, bf16[128,1024]{1,0:T(8,128)(2,1)},...) custom-call(s32[32]{0:T(128)} %rp_ref.1, bf16[128,4096]{1,0:T(8,128)(2,1)} %bitcast.8, ...), custom_call_target="tpu_custom_call" | custom-call | tf_op jit(solution)/shard_map/attention_step/pallas_call | solution.py:514
  95.6 4.0 %finish.1 = (bf16[128,4096]{1,0:T(8,128)(2,1)}, bf16[128,4096]{1,0:T(8,128)(2,1)}, bf16[128,1024]{1,0:T(8,128)(2,1)}, bf16[128,1024]{1,0:T(8,128)(2,1)}, bf16[2,...) custom-call(bf16[128,4096]{1,0:T(8,128)(2,1)} %get-tuple-element.18.refs_0_, ...), custom_call_target="tpu_custom_call" | custom-call | tf_op jit(solution)/shard_map/finish/pallas_call | solution.py:580

commit v3 on v2

--- a/solution.py
+++ b/solution.py
@@ -11,6 +11,7 @@
 BF16 = jnp.bfloat16
 HD = 128
 SPAN = 128
+PART = 128
 SCALING = 1.0 / math.sqrt(HD)
 SCALING2 = SCALING * math.log2(math.e)
 MESH = pl.DeviceIdType.MESH
@@ -25,44 +26,53 @@
 
 
 def head_pass(h, valid, between, qb, db, kv, gacc, ob, qgb, s_scr, d_scr):
-    row = lax.broadcasted_iota(jnp.int32, (256, 256), 0)
-    col = lax.broadcasted_iota(jnp.int32, (256, 256), 1)
-    keep = row <= col
+    row = lax.broadcasted_iota(jnp.int32, (PART, 256), 0)
+    col = lax.broadcasted_iota(jnp.int32, (PART, 256), 1)
     for g in range(4):
         lanes = slice(g * HD, (g + 1) * HD)
         slot = g % 2
         qg = qb[h, :, :, lanes].reshape(256, HD)
         dog = db[h, :, :, lanes].reshape(256, HD)
-        top = None
+        tops, totals, centres = [], [], []
         for j in range(8):
-            s = dot(kv[h, j, 0], qg, NT) * SCALING2
-            if j == 4:
-                s = jnp.where(keep, s, -jnp.inf)
-            s_scr[slot, j] = s
-            top_j = jnp.max(s, axis=0, keepdims=True)
-            if j > 4:
-                top_j = jnp.where(valid[j - 4], top_j, -jnp.inf)
-            top = top_j if top is None else jnp.maximum(top, top_j)
-        total = None
-        centre = None
-        for j in range(8):
-            shift = top if j <= 4 else jnp.where(valid[j - 4], top, jnp.inf)
-            w = jnp.exp2(s_scr[slot, j] - shift)
-            dp = dot(kv[h, j, 1], dog, NT)
-            s_scr[slot, j] = w
-            d_scr[slot, j] = dp
-            total_j = jnp.sum(w, axis=0, keepdims=True)
-            centre_j = jnp.sum(w * dp, axis=0, keepdims=True)
-            total = total_j if total is None else total + total_j
-            centre = centre_j if centre is None else centre + centre_j
+            for at in range(0, 256, PART):
+                part = slice(at, at + PART)
+                s = dot(kv[h, j, 0, part], qg, NT) * SCALING2
+                if j == 4:
+                    s = jnp.where(row + at <= col, s, -jnp.inf)
+                top = jnp.max(s, axis=0, keepdims=True)
+                if j == 4:
+                    top = jnp.maximum(top, -1e30)
+                w = jnp.exp2(s - top)
+                dp = dot(kv[h, j, 1, part], dog, NT)
+                s_scr[slot, j, part] = w
+                d_scr[slot, j, part] = dp
+                tops.append(top if j <= 4 else jnp.where(valid[j - 4], top, -jnp.inf))
+                totals.append(jnp.sum(w, axis=0, keepdims=True))
+                centres.append(jnp.sum(w * dp, axis=0, keepdims=True))
+        row_top = tops[0]
+        for top in tops[1:]:
+            row_top = jnp.maximum(row_top, top)
+        factors = [jnp.exp2(top - row_top) for top in tops]
+        total = factors[0] * totals[0]
+        centre = factors[0] * centres[0]
+        for n in range(1, len(factors)):
+            total = total + factors[n] * totals[n]
+            centre = centre + factors[n] * centres[n]
         inv = 1.0 / total
         centre = centre * inv
+        factors = [factor * inv for factor in factors]
         out_t = None
         qgrad_t = None
         for j in range(8):
-            probs = s_scr[slot, j] * inv
-            score_grad = (probs * (d_scr[slot, j] - centre)).astype(BF16)
-            probs_low = probs.astype(BF16)
+            lows, grads = [], []
+            for n in range(256 // PART):
+                part = slice(n * PART, (n + 1) * PART)
+                probs = s_scr[slot, j, part] * factors[j * (256 // PART) + n]
+                grads.append((probs * (d_scr[slot, j, part] - centre)).astype(BF16))
+                lows.append(probs.astype(BF16))
+            probs_low = jnp.concatenate(lows, axis=0)
+            score_grad = jnp.concatenate(grads, axis=0)
             dv = dot(probs_low, dog, NN)
             dk = dot(score_grad, qg, NN)
             if g == 0:
@@ -273,6 +283,10 @@
     send_plane(0)
     send_keys(0, 2)
     send_keys(0, 3)
+    send_plane(1)
+    send_inputs(1)
+    send_keys(1, 2)
+    send_keys(1, 3)
     hand_on(0)
 
     valid = [chip >= d for d in range(4)]
@@ -289,18 +303,17 @@
 
         wait_for(kv.at[h, pl.ds(0, 4)], r_p.at[h])
 
-        @pl.when(step == 0)
-        def _():
-            send_plane(1)
-            send_inputs(1)
+        @pl.when(step < 2)
+        def _():
+            send_plane(step + 2)
+            send_inputs(step + 2)
+            send_keys(step + 2, 2)
+            send_keys(step + 2, 3)
 
         def between(g):
             if g == 0:
 
-                @pl.when(step == 0)
-                def _():
-                    send_keys(1, 2)
-                    send_keys(1, 3)
+                pass
             elif g == 1:
 
                 @pl.when(step < 3)
@@ -308,36 +321,31 @@
                     hand_on(step + 1)
             elif g == 2:
 
-                @pl.when(step < 2)
-                def _():
-                    send_plane(step + 2)
-                    send_inputs(step + 2)
-                    send_keys(step + 2, 2)
-                    send_keys(step + 2, 3)
-
                 @pl.when(step > 0)
                 def _():
                     merge(step - 1)
 
         head_pass(h, valid, between, qb, db, kv, gacc, ob, qgb, s_scr, d_scr)
-        for j in range(4):
-            st[h, j, 0] = (gacc[j, 0] * SCALING).astype(BF16)
-            st[h, j, 1] = gacc[j, 1].astype(BF16)
         head = core * 4 + h
-        for x in range(2):
-            for k in range(2):
-                here = (head == resp) & (x == x_lo) & (k == core)
-                src = st.at[h, x * 2 + k]
-
-                @pl.when(here)
-                def _():
-                    pltpu.make_async_copy(src, ar.at[plane], r_a).start()
-
-                @pl.when(jnp.logical_not(here))
-                def _():
-                    remote(
-                        src, ar.at[plane], s_a.at[h, x * 2 + k], r_a, seq_of(x, z, k), head
-                    ).start()
+        for which in range(2):
+            for x in range(2):
+                for k in range(2):
+                    n = x * 2 + k
+                    term = gacc[n, which]
+                    st[h, n, which] = (term * SCALING if which == 0 else term).astype(BF16)
+                    here = (head == resp) & (x == x_lo) & (k == core)
+                    src = st.at[h, n, which]
+                    dst = ar.at[plane, which]
+
+                    @pl.when(here)
+                    def _():
+                        pltpu.make_async_copy(src, dst, r_a.at[which]).start()
+
+                    @pl.when(jnp.logical_not(here))
+                    def _():
+                        remote(
+                            src, dst, s_a.at[which, h, n], r_a.at[which], seq_of(x, z, k), head
+                        ).start()
 
         def send_terms(d):
             for k in range(2):
@@ -394,34 +402,36 @@
 
     merge(3)
 
-    wait_for(ar, r_a)
     second = [rp_ref[(a // 2) * 4 + (a % 2) * 2 + z_hi] == 1 for a in range(16)]
 
-    def sum_plane(t, _):
-        to = (z + t) % 8
-        rows = pl.ds(pl.multiple_of(to * 32, 32), 32)
-        for which in range(2):
+    for which in range(2):
+        wait_for(ar.at[:, which], r_a.at[which])
+
+        def sum_plane(t, _, which=which):
+            to = (z + t) % 8
+            rows = pl.ds(pl.multiple_of(to * 32, 32), 32)
             sums = [jnp.zeros((32, HD), F32), jnp.zeros((32, HD), F32)]
             for a in range(16):
                 term = ar[a, which, rows].astype(F32)
                 sums[0] += jnp.where(second[a], 0.0, term)
                 sums[1] += jnp.where(second[a], term, 0.0)
             for p in range(2):
-                zs[to, p, which] = sums[p].astype(BF16)
-
-        @pl.when(t == 0)
-        def _():
-            pltpu.make_async_copy(zs.at[to], zr.at[z], r_zz).start()
-
-        @pl.when(t > 0)
-        def _():
-            remote(
-                zs.at[to], zr.at[z], s_zz, r_zz, seq_of(x_lo, to, core), resp
-            ).start()
-
-        return 0
-
-    lax.fori_loop(0, 8, sum_plane, 0)
+                zs[which, to, p] = sums[p].astype(BF16)
+
+            @pl.when(t == 0)
+            def _():
+                pltpu.make_async_copy(zs.at[which, to], zr.at[which, z], r_zz.at[which]).start()
+
+            @pl.when(t > 0)
+            def _():
+                remote(
+                    zs.at[which, to], zr.at[which, z], s_zz, r_zz.at[which],
+                    seq_of(x_lo, to, core), resp,
+                ).start()
+
+            return 0
+
+        lax.fori_loop(0, 8, sum_plane, 0)
 
     wait_for(gr.at[0], r_g.at[0])
     racc[...] = gr[0].astype(F32)
@@ -436,27 +446,29 @@
         rkg_ref[:, n * HD : (n + 1) * HD] = racc[n, 0].astype(BF16)
         rvg_ref[:, n * HD : (n + 1) * HD] = racc[n, 1].astype(BF16)
 
-    wait_for(zr, r_zz)
     for which in range(2):
+        wait_for(zr.at[which], r_zz.at[which])
         for p in range(2):
-            final = zr[0, p, which].astype(F32)
+            final = zr[which, 0, p].astype(F32)
             for n in range(1, 8):
-                final = final + zr[n, p, which].astype(F32)
+                final = final + zr[which, n, p].astype(F32)
             fo[which, p] = final.astype(BF16)
-    pltpu.make_async_copy(fo, fr.at[resp], r_f).start()
-
-    def send_replica(t, _):
-        remote(fo, fr.at[resp], s_f, r_f, seq, (resp + t) % 8).start()
-        return 0
-
-    lax.fori_loop(1, 8, send_replica, 0)
+        pltpu.make_async_copy(fo.at[which], fr.at[which, resp], r_f.at[which]).start()
+
+        def send_replica(t, _, which=which):
+            remote(
+                fo.at[which], fr.at[which, resp], s_f, r_f.at[which], seq, (resp + t) % 8
+            ).start()
+            return 0
+
+        lax.fori_loop(1, 8, send_replica, 0)
 
     wait_for(o_ref, r_o)
     wait_for(qg_ref, r_qg)
-    wait_for(fr, r_f)
-    for n in range(8):
-        pkg_ref[:, :, n * HD : (n + 1) * HD] = fr[n, 0]
-        pvg_ref[:, :, n * HD : (n + 1) * HD] = fr[n, 1]
+    for which, dst in enumerate((pkg_ref, pvg_ref)):
+        wait_for(fr.at[which], r_f.at[which])
+        for n in range(8):
+            dst[:, :, n * HD : (n + 1) * HD] = fr[which, n]
 
     wait_for(relay.at[pl.ds(0, 7)], s_z)
     for at in range(16):
@@ -493,10 +505,11 @@
 
             @pl.when(jnp.logical_not(here))
             def _():
-                wait_for(st.at[h, n], s_a.at[h, n])
-
-    wait_for(zr.at[pl.ds(0, 7)], s_zz)
-    wait_for(fr.at[pl.ds(0, 7)], s_f)
+                for which in range(2):
+                    wait_for(st.at[h, n, which], s_a.at[which, h, n])
+
+    wait_for(zr.at[:, pl.ds(0, 7)], s_zz)
+    wait_for(fr.at[:, pl.ds(0, 7)], s_f)
 
 
 def finish(*refs):
@@ -529,10 +542,10 @@
             pltpu.VMEM((4, 2, SPAN, 512), BF16),
             pltpu.VMEM((4, 2, SPAN, 512), BF16),
             pltpu.VMEM((16, 2, 256, HD), BF16),
-            pltpu.VMEM((8, 2, 2, 32, HD), BF16),
-            pltpu.VMEM((8, 2, 2, 32, HD), BF16),
+            pltpu.VMEM((2, 8, 2, 32, HD), BF16),
+            pltpu.VMEM((2, 8, 2, 32, HD), BF16),
             pltpu.VMEM((2, 2, 32, HD), BF16),
-            pltpu.VMEM((8, 2, 2, 32, HD), BF16),
+            pltpu.VMEM((2, 8, 2, 32, HD), BF16),
             pltpu.VMEM((4, 8, 2, SPAN, HD), BF16),
             pltpu.VMEM((4, 2, 2, SPAN, HD), BF16),
             pltpu.VMEM((8, 2, SPAN, HD), F32),
@@ -548,9 +561,9 @@
             dma(()),
             dma((4,)),
             dma((4,)),
-            dma(()),
-            dma(()),
-            dma(()),
+            dma((2,)),
+            dma((2,)),
+            dma((2,)),
             dma(()),
             dma((16,)),
             dma((4,)),
@@ -560,7 +573,7 @@
             dma(()),
             dma(()),
             dma((4,)),
-            dma((4, 4)),
+            dma((2, 4, 4)),
             dma(()),
             dma(()),
         ],

time: 102 us -> 97.3 us (0.954)
  Pallas kernels: 99 us -> 95 us
    pallas_call x1, Pallas kernels: 95 us -> 91 us  [body(): pl.pallas_call(kernel, out_shape=(rows, rows, block, block, shard, shard)...]
where the time goes in v3:
time: 97.3 us; the launch traced here: 95.7 us
  Pallas kernels  95 us (98%)
    pallas_call x1, Pallas kernels, body(): pl.pallas_call(kernel, out_shape=(rows, rows, block, block, shard, shard)...  91 us
    pallas_call x1, Pallas kernels, body(): pl.pallas_call(finish, out_shape=(rows, rows, block, block, shard, shard)...  4.03 us

profile of v3, /device:TPU:6, one launch (start us, length us, event | category | flops | bytes accessed | tf_op | source)
XLA Modules:
  0.0 95.7 jit_solution(2662763969833379354)
XLA Ops:
  0.6 91.0 %attention_step.1 = (bf16[128,4096]{1,0:T(8,128)(2,1)}, bf16[128,4096]{1,0:T(8,128)(2,1)}, bf16[128,1024]{1,0:T(8,128)(2,1)}, bf16[128,1024]{1,0:T(8,128)(2,1)},...) custom-call(s32[32]{0:T(128)} %rp_ref.1, bf16[128,4096]{1,0:T(8,128)(2,1)} %bitcast.8, ...), custom_call_target="tpu_custom_call" | custom-call | tf_op jit(solution)/shard_map/attention_step/pallas_call | solution.py:527
  91.6 4.0 %finish.1 = (bf16[128,4096]{1,0:T(8,128)(2,1)}, bf16[128,4096]{1,0:T(8,128)(2,1)}, bf16[128,1024]{1,0:T(8,128)(2,1)}, bf16[128,1024]{1,0:T(8,128)(2,1)}, bf16[2,...) custom-call(bf16[128,4096]{1,0:T(8,128)(2,1)} %get-tuple-element.18.refs_0_, ...), custom_call_target="tpu_custom_call" | custom-call | tf_op jit(solution)/shard_map/finish/pallas_call | solution.py:593
